TPU v7x, 128 devices: a whole 4x4x4 slice. The times are simulated.
128 devices in a mesh: row: 16 (over z, y), col: 8 (over x, core).
Axes of the slice: x: 4, y: 4, z: 4, core: 2. Of those that a mesh axis runs over, the one named last changes fastest.
Arguments:
- child_fronts: float32 [128, 2048, 2048], P(('row', 'col')), may hold values from -3 to 20, as said below
- child_tiles: int32 [128, 12], P(('row', 'col')), may hold values from 0 to 63, as said below
- parent_front: float32 [8192, 8192], P('row', 'col'), may hold values from -5 to 20, as said below
Outputs:
- child_factors: float32 [128, 2048, 512], P(('row', 'col'))
- parent_result: float32 [8192, 8192], P('row', 'col')
Inputs may be any that keep to these rules, and one draw needn't show every extreme that they name: `child_tiles`: each row holds strictly increasing parent tile indices, no two of them in the same group of 4 consecutive tiles. `child_fronts`: each child front is symmetric positive definite. `parent_front`: symmetric positive definite.
All inputs are finite; a program needn't handle non-finite values.
Results may differ from a plain program's by a relative error of at most 0.0003.
Values sent between devices are 32-bit elements; how exact they have to be, the bound alone decides.
No kernel may reach another device: no remote copies, remote signals or barrier semaphores. Data moves between devices by JAX's collectives and lax.ppermute only.
A program may use at most 192 MiB of HBM per device.

v0:
```python
import jax
import jax.numpy as jnp
from jax import lax
from jax.sharding import PartitionSpec as P

PANEL = 512
TILE = 128
CP = 512
PANELS = 2
TPB = 4
NB = 16
CT = 12
PRECISE = lax.Precision.HIGHEST


def from_root(value, axis, source):
    kept = jnp.where(lax.axis_index(axis) == source, value, 0).astype(value.dtype)
    return lax.psum(kept, axis)


def product(left_side, right_side):
    return lax.dot_general(
        left_side,
        right_side,
        (((1,), (1,)), ((), ())),
        precision=PRECISE,
        preferred_element_type=jnp.float32,
    )


def right_solve(factor, right_block):
    return jax.scipy.linalg.solve_triangular(factor, right_block.T, lower=True).T


def eliminate_child(matrix):
    corner = jnp.linalg.cholesky(matrix[:CP, :CP])
    below_rows = right_solve(corner, matrix[CP:, :CP])
    update = matrix[CP:, CP:] - product(below_rows, below_rows)
    return (jnp.concatenate([corner, below_rows], axis=0), update)


def keep_blocks(panel_block, block_ids, pivot_step, corner):
    block_count = block_ids.shape[0]
    stacked = panel_block.reshape(block_count, PANEL, PANEL)
    chosen = jnp.where((block_ids > pivot_step)[:, None, None], stacked, 0.0)
    chosen = jnp.where((block_ids == pivot_step)[:, None, None], corner[None], chosen)
    return chosen.reshape(block_count * PANEL, PANEL)


def locate(everyone, targets):
    matches = (everyone // TPB)[:, :, None] == targets[None, None, :]
    located = jnp.any(matches, axis=1)
    offset_in = jnp.sum(jnp.where(matches, (everyone % TPB)[:, :, None], 0), axis=1)
    return (located, offset_in)


def on_device(child_fronts, child_tiles, parent_front):
    row_count = lax.axis_size("row")
    col_count = lax.axis_size("col")
    row_ratio = row_count // col_count
    row_blocks = parent_front.shape[0] // PANEL
    col_blocks = parent_front.shape[1] // PANEL
    slot_count = row_blocks * col_blocks
    devices_all = row_count * col_count
    factor, update = eliminate_child(child_fronts[0])
    indices = child_tiles[0]
    block_ids = jnp.arange(NB, dtype=jnp.int32)
    matches = (indices // TPB)[None, :] == block_ids[:, None]
    present = jnp.any(matches, axis=1)
    source_tile = jnp.sum(jnp.where(matches, jnp.arange(CT, dtype=jnp.int32)[None, :], 0), axis=1)
    picked_rows = (
        source_tile[:, None] * TILE + jnp.arange(TILE, dtype=jnp.int32)[None, :]
    ).reshape(-1)
    spread = jnp.take(jnp.take(update, picked_rows, axis=0), picked_rows, axis=1)
    spread = spread.reshape(NB, TILE, NB, TILE)
    spread = jnp.where((present[:, None] & present[None, :])[:, None, :, None], spread, 0.0)
    outgoing = spread.reshape(row_count, row_blocks, TILE, col_count, col_blocks, TILE)
    outgoing = outgoing.transpose(0, 3, 1, 4, 2, 5).reshape(
        row_count, col_count, slot_count, TILE, TILE
    )
    arrived = lax.all_to_all(
        outgoing.reshape(devices_all, slot_count, TILE, TILE),
        ("row", "col"),
        split_axis=0,
        concat_axis=0,
        tiled=True,
    )
    arrived = arrived.reshape(devices_all * slot_count, TILE * TILE)
    everyone = lax.all_gather(child_tiles, ("row", "col"), axis=0, tiled=True)
    row_index = lax.axis_index("row")
    col_index = lax.axis_index("col")
    own_rows = row_index * row_blocks + jnp.arange(row_blocks, dtype=jnp.int32)
    own_cols = col_index * col_blocks + jnp.arange(col_blocks, dtype=jnp.int32)
    found_rows, offset_rows = locate(everyone, own_rows)
    found_cols, offset_cols = locate(everyone, own_cols)
    row_spot = jnp.arange(row_blocks, dtype=jnp.int32)[None, :] * TPB + offset_rows
    col_spot = jnp.arange(col_blocks, dtype=jnp.int32)[None, :] * TPB + offset_cols
    target_spots = row_spot[:, :, None] * (col_blocks * TPB) + col_spot[:, None, :]
    target_spots = jnp.where(
        found_rows[:, :, None] & found_cols[:, None, :], target_spots, -1
    ).reshape(-1)
    places = row_blocks * TPB * col_blocks * TPB
    chooser = (jnp.arange(places, dtype=jnp.int32)[:, None] == target_spots[None, :]).astype(
        jnp.float32
    )
    summed = jnp.dot(chooser, arrived, precision=PRECISE, preferred_element_type=jnp.float32)
    summed = summed.reshape(row_blocks * TPB, col_blocks * TPB, TILE, TILE).transpose(0, 2, 1, 3)
    assembled = parent_front + summed.reshape(parent_front.shape)
    identity = jnp.eye(PANEL, dtype=jnp.float32)
    for pivot_step in range(PANELS):
        row_slot = pivot_step % row_blocks
        col_slot = pivot_step % col_blocks
        owner_row = pivot_step // row_blocks
        owner_col = pivot_step // col_blocks
        column_block = assembled[:, col_slot * PANEL : (col_slot + 1) * PANEL]
        candidate = column_block
        holder = (row_index == owner_row) & (col_index == owner_col)
        candidate = jnp.where(holder, candidate, identity)
        corner = from_root(jnp.linalg.cholesky(candidate), "row", owner_row)
        panel_rows = keep_blocks(right_solve(corner, column_block), own_rows, pivot_step, corner)
        panel_rows = from_root(panel_rows, "col", owner_col)
        pieces = []
        for member in range(row_ratio):
            pieces.append(from_root(panel_rows, "row", col_index * row_ratio + member))
        panel_cols = jnp.concatenate(pieces, axis=0)
        change = product(panel_rows, panel_cols)
        row_live = jnp.repeat(own_rows > pivot_step, PANEL)
        col_live = jnp.repeat(own_cols > pivot_step, PANEL)
        row_here = jnp.repeat(own_rows == pivot_step, PANEL)
        col_here = jnp.repeat(own_cols == pivot_step, PANEL)
        renewed = jnp.where(row_live[:, None] & col_live[None, :], assembled - change, assembled)
        renewed = jnp.where(row_here[:, None] & col_live[None, :], 0.0, renewed)
        assembled = jnp.where(col_here[None, :], jnp.tile(panel_rows, (1, col_blocks)), renewed)
    return (factor[None], assembled)


def solution(mesh):
    placed = (P(("row", "col"), None, None), P(("row", "col"), None), P("row", "col"))
    return jax.shard_map(
        on_device,
        mesh=mesh,
        in_specs=placed,
        out_specs=(P(("row", "col"), None, None), P("row", "col")),
        check_vma=False,
    )
```

profile of v0, /device:TPU:0, one launch (start us, length us, event | category | flops | bytes accessed | tf_op | source)
XLA Modules:
  0.0 1473.7 jit_solution(17172467723713971530)
XLA Ops:
  7.2 17.6 %copy.75 = f32[1,2048,2048]{1,2,0:T(8,128)} copy(f32[1,2048,2048]{2,1,0:T(8,128)} %param.6) | data formatting | bytes 33554432 | tf_op args[0]
  35.0 11.7 cholesky.374
  60.8 11.7 cholesky.393
  85.5 11.7 cholesky.414
  110.7 12.1 cholesky.431
  142.0 40.1 %custom-call.27 = f32[4,128,128]{1,2,0:T(8,128)S(1)} custom-call(f32[4,128,128]{2,1,0:T(8,128)} %copy-done.22), custom_call_target="InvertDiagBlocksLowerTriangular" | custom-call | tf_op jit(solution)/shard_map/jit(_solve_triangular)/triangular_solve | solution.py:32
  193.0 19.6 %slice_subtract_fusion = f32[1536,1536]{0,1:T(8,128)} fusion(f32[2048,2048]{0,1:T(8,128)} %bitcast.231, f32[128,1536]{1,0:T(8,128)S(1)} %fusion.93, f32[128,1536]{1,0:T(8,128)S(1)} %fusion.94, f32[128,1536]{1,0:T(8,128)S(1)} %fusion.96, f32[128,1536]{1,0:T(8,128)S(1)} %fusion.35), kind=kOutput, calls=%fused_computation.10 | convolution fusion | flops 14500233216 | bytes 22020096 | tf_op jit(solution)/shard_map/dot_general | solution.py:22
  222.2 18.0 %gather_fusion = f32[2048,1536]{1,0:T(8,128)} fusion(f32[1536,1536]{1,0:T(8,128)} %copy.84, s32[2048]{0:T(1024)S(1)} %broadcast_clamp_fusion), kind=kCustom, calls=%fused_computation | custom fusion | bytes 25174016 | tf_op jit(solution)/shard_map/jit(_take)/gather | solution.py:74
  250.1 12.6 copy.85
  262.7 21.1 %gather_fusion.1 = f32[2048,2048]{1,0:T(8,128)} fusion(f32[2048,1536]{0,1:T(8,128)} %copy.85, s32[2048]{0:T(1024)S(1)} %broadcast_clamp_fusion), kind=kCustom, calls=%fused_computation.1 | custom fusion | bytes 33562624 | tf_op jit(solution)/shard_map/jit(_take)/gather | solution.py:74
  283.8 14.2 copy.126
  298.0 17.7 %copy.86 = f32[16,1,128,8,2,128]{5,2,4,3,0,1:T(8,128)} copy(f32[16,1,128,8,2,128]{2,0,5,4,3,1:T(8,128)} %bitcast.226) | data formatting | bytes 33554432 | tf_op jit(solution)/shard_map/jit(_take)/gather | solution.py:74
  327.6 11.7 all-to-all-start
  339.3 263.6 %all-gather = s32[128,1,12]{2,1,0:T(1,128)S(1)} all-gather(s32[1,1,12]{2,1,0:T(1,128)S(1)} %bitcast.237), channel_id=1, replica_groups=mesh['row'=16,'col'=8] {'row','col'}, dimensions={0}, use_global_device_ids=true | all-gather | bytes 6192 | tf_op jit(solution)/shard_map/all_gather | solution.py:89
  606.6 18.4 %copy.131 = f32[32,8,128,128]{3,1,2,0:T(8,128)} copy(f32[32,8,128,128]{3,2,1,0:T(8,128)} %bitcast.82) | data formatting | bytes 33554432
  625.0 17.5 %copy.87 = f32[16384,256]{1,0:T(8,128)} copy(f32[16384,256]{0,1:T(8,128)} %bitcast.227) | data formatting | bytes 33554432 | tf_op jit(solution)/shard_map/dot_general | solution.py:106
  664.1 11.7 cholesky.446
  688.3 11.7 cholesky.465
  712.9 11.7 cholesky.486
  736.6 12.1 cholesky.503
  753.0 83.4 %all-reduce.10.cloned.1.call-done = f32[512,512]{1,0:T(8,128)} async-done(((f32[512,512]{1,0:T(8,128)}), f32[512,512]{1,0:T(8,128)}) %all-reduce.10.cloned.1.call-update) | async-done | bytes 1048592 | tf_op jit(solution)/shard_map/psum | solution.py:18
  850.0 39.9 %custom-call.41 = f32[4,128,128]{1,2,0:T(8,128)} custom-call(f32[4,128,128]{2,1,0:T(8,128)S(1)} %get-tuple-element.26), custom_call_target="InvertDiagBlocksLowerTriangular" | custom-call | tf_op jit(solution)/shard_map/jit(_solve_triangular)/triangular_solve | solution.py:32
  908.1 61.6 %all-reduce.12.cloned.1.call-done = f32[512,512]{1,0:T(8,128)} async-done(((f32[512,512]{1,0:T(8,128)}), f32[512,512]{1,0:T(8,128)}) %all-reduce.12.cloned.1.call-update) | async-done | bytes 1048592 | tf_op jit(solution)/shard_map/psum | solution.py:18
  974.3 89.1 %all-reduce.20.cloned.1.call-done = (f32[512,512]{1,0:T(8,128)}, f32[512,512]{1,0:T(8,128)}) async-done(((f32[512,512]{1,0:T(8,128)}, f32[512,512]{1,0:T(8,128)}), (f32[512,512]{1,0:T(8,128)}, f32[512,512]{1,0:T(8,128)})) %all-reduce.20.cloned.1.call-update) | async-done | bytes 2097168 | tf_op jit(solution)/shard_map/psum | solution.py:18
  1072.2 11.7 cholesky.518
  1096.4 11.9 cholesky.537
  1121.1 11.7 cholesky.558
  1144.9 11.7 cholesky.575
  1161.0 86.7 %all-reduce.14.cloned.1.call-done = f32[512,512]{1,0:T(8,128)} async-done(((f32[512,512]{1,0:T(8,128)}), f32[512,512]{1,0:T(8,128)}) %all-reduce.14.cloned.1.call-update) | async-done | bytes 1048592 | tf_op jit(solution)/shard_map/psum | solution.py:18
  1257.3 39.3 %custom-call.45 = f32[4,128,128]{1,2,0:T(8,128)S(1)} custom-call(f32[4,128,128]{2,1,0:T(8,128)S(1)} %get-tuple-element.27), custom_call_target="InvertDiagBlocksLowerTriangular" | custom-call | tf_op jit(solution)/shard_map/jit(_solve_triangular)/triangular_solve | solution.py:32
  1301.8 61.3 %all-reduce.16.cloned.1.call-done = f32[512,512]{1,0:T(8,128)} async-done(((f32[512,512]{1,0:T(8,128)}), f32[512,512]{1,0:T(8,128)}) %all-reduce.16.cloned.1.call-update) | async-done | bytes 1048592 | tf_op jit(solution)/shard_map/psum | solution.py:18
  1379.1 77.5 %all-reduce.18.cloned.1.call-done = (f32[512,512]{1,0:T(8,128)}, f32[512,512]{1,0:T(8,128)}) async-done(((f32[512,512]{1,0:T(8,128)}, f32[512,512]{1,0:T(8,128)}), (f32[512,512]{1,0:T(8,128)}, f32[512,512]{1,0:T(8,128)})) %all-reduce.18.cloned.1.call-update) | async-done | bytes 2097168 | tf_op jit(solution)/shard_map/psum | solution.py:18
  (282 shorter events, 328.8 us)
Async XLA Ops:
  27.1 2.1 copy-start.25
  34.0 1.0 copy-start.19
  142.0 45.6 %copy-start.23 = (s32[4,2]{0,1:T(2,128)}, s32[4,2]{0,1:T(2,128)S(1)}, u32[]{:S(2)}) copy-start(s32[4,2]{0,1:T(2,128)S(1)} %get-tuple-element.299) | copy-start | bytes 100
  183.0 9.1 copy-start
  185.6 6.5 copy-start.2
  188.5 3.6 copy-start.6
  192.1 0.9 copy-start.10
  327.6 277.2 %copy-start.21 = (f32[512,1024]{1,0:T(8,128)S(1)}, f32[512,1024]{1,0:T(8,128)}, u32[]{:S(2)}) copy-start(f32[512,1024]{1,0:T(8,128)} %param.8) | copy-start | bytes 6291460
  327.6 279.0 %all-to-all-start = ((f32[128,2,128,128]{3,2,1,0:T(8,128)}), f32[128,2,128,128]{3,2,1,0:T(8,128)}, u32[]{:S(2)}, u32[]{:S(2)}) async-start(f32[128,2,128,128]{3,2,1,0:T(8,128)} %bitcast.224), calls=%async_computation | async-start | bytes 33554432 | tf_op jit(solution)/shard_map/all_to_all | solution.py:81
  339.3 497.2 %all-reduce.10.cloned.1.call-start = ((), (), s32[]{:S(2)}) async-start(), calls=%async_computation.1 | async-start | bytes 2097152 | tf_op jit(solution)/shard_map/psum | solution.py:18
  663.1 1.0 copy-start.17
  724.7 114.1 %copy-start.24 = (s32[4,2]{0,1:T(2,128)S(1)}, s32[4,2]{0,1:T(2,128)}, u32[]{:S(2)}) copy-start(s32[4,2]{0,1:T(2,128)} %copy-done.23) | copy-start | bytes 100
  752.9 137.0 %copy-start.14 = (f32[512,512]{1,0:T(8,128)S(1)}, f32[512,512]{1,0:T(8,128)}, u32[]{:S(2)}) copy-start(f32[512,512]{1,0:T(8,128)} %get-tuple-element.78) | copy-start | bytes 3145732
  752.9 216.7 %all-reduce.12.cloned.1.call-start = ((), (), s32[]{:S(2)}) async-start(), calls=%async_computation.2 | async-start | bytes 2097152 | tf_op jit(solution)/shard_map/psum | solution.py:18
  892.4 13.3 copy-start.13
  893.8 2.8 copy-start.15
  896.6 0.7 copy-start.20
  908.0 155.4 %all-reduce.20.cloned.1.call-start = ((), (), s32[]{:S(2)}) async-start(), calls=%async_computation.6 | async-start | bytes 4194304 | tf_op jit(solution)/shard_map/psum | solution.py:18
  969.7 3.3 copy-start.9
  972.6 275.1 %all-reduce.14.cloned.1.call-start = ((), (), s32[]{:S(2)}) async-start(), calls=%async_computation.3 | async-start | bytes 2097152 | tf_op jit(solution)/shard_map/psum | solution.py:18
  1069.1 1.3 copy-start.4
  1071.2 1.0 copy-start.18
  1160.9 202.1 %all-reduce.16.cloned.1.call-start = ((), (), s32[]{:S(2)}) async-start(), calls=%async_computation.4 | async-start | bytes 2097152 | tf_op jit(solution)/shard_map/psum | solution.py:18
  1298.7 1.5 copy-start.12
  1301.5 67.3 %copy-start.1 = (f32[128,1536]{1,0:T(8,128)S(1)}, f32[128,1536]{1,0:T(8,128)}, u32[]{:S(2)}) copy-start(f32[128,1536]{1,0:T(8,128)} %copy-done) | copy-start | bytes 2359300
  1301.5 67.3 %copy-start.3 = (f32[128,1536]{1,0:T(8,128)S(1)}, f32[128,1536]{1,0:T(8,128)}, u32[]{:S(2)}) copy-start(f32[128,1536]{1,0:T(8,128)} %copy-done.2) | copy-start | bytes 2359300
  1301.5 67.3 %copy-start.7 = (f32[128,1536]{1,0:T(8,128)S(1)}, f32[128,1536]{1,0:T(8,128)}, u32[]{:S(2)}) copy-start(f32[128,1536]{1,0:T(8,128)} %copy-done.6) | copy-start | bytes 2359300
  1301.5 67.3 %copy-start.11 = (f32[128,1536]{1,0:T(8,128)S(1)}, f32[128,1536]{1,0:T(8,128)}, u32[]{:S(2)}) copy-start(f32[128,1536]{1,0:T(8,128)} %copy-done.10) | copy-start | bytes 2359300
  1301.5 155.1 %all-reduce.18.cloned.1.call-start = ((), (), s32[]{:S(2)}) async-start(), calls=%async_computation.5 | async-start | bytes 4194304 | tf_op jit(solution)/shard_map/psum | solution.py:18
  1368.8 1.2 copy-start.16
  1372.4 5.5 copy-start.8
  1377.8 78.8 %copy-start.5 = (f32[512,1024]{0,1:T(8,128)S(1)}, f32[512,1024]{0,1:T(8,128)}, u32[]{:S(2)}) copy-start(f32[512,1024]{0,1:T(8,128)} %copy-done.4) | copy-start | bytes 6291460
  (1 other events, 0.7 us)
Sparse Core Ops, SparseCore 0:
  753.0 83.3 all-reduce.9
  908.2 61.4 all-reduce.11
  973.6 89.7 all-reduce.19
  1161.1 86.5 all-reduce.13
  1301.6 61.4 all-reduce.15
  1366.7 89.8 all-reduce.17
where the time goes:
time: 1490 us; the launch traced here: 1470 us
  waiting for transfers between devices  460 us (31%)
  other arithmetic  410 us (28%)
  blocking collectives  264 us (18%)
  local copies, waits for them, and re-layouts  219 us (15%)
  matrix products  85.5 us (6%)
  between operations  23 us (2%)
    psum x6, waiting for transfers between devices, from_root(): return lax.psum(kept, axis)  460 us
    all_gather x1, blocking collectives, on_device(): everyone = lax.all_gather(child_tiles, ('row', 'col'), axis=0, tiled=True)  264 us
    another operation x30, other arithmetic, on_device(): corner = from_root(jnp.linalg.cholesky(candidate), 'row', owner_row)  159 us
    another operation x7, other arithmetic, right_solve(): jax.scipy.linalg.solve_triangular(factor, right_block.T, lower=True)  126 us
    another operation x14, other arithmetic, eliminate_child(): corner = jnp.linalg.cholesky(matrix[:CP, :CP])  80.8 us
    unnamed x62, local copies, waits for them, and re-layouts  68.5 us
    gather x2, local copies, waits for them, and re-layouts, on_device(): jnp.take(jnp.take(update, picked_rows, axis=0), picked_rows, axis=1)  38.8 us
    dot_general x3, matrix products, product(): lax.dot_general(left_side, right_side, (((1,), (1,)), ((), ())), precisio...  32.1 us
  transfers between devices with their start and end apart: 7, of which 6 were waited for; matrix products, arithmetic and copies ran while one was open for 1% of the time, Pallas kernels for 0%

commit v1 on v0

--- a/solution.py
+++ b/solution.py
@@ -15,7 +15,7 @@
 
 def from_root(value, axis, source):
     kept = jnp.where(lax.axis_index(axis) == source, value, 0).astype(value.dtype)
-    return lax.psum(kept, axis)
+    return jnp.sum(lax.all_gather(kept, axis), axis=0)
 
 
 def product(left_side, right_side):

time: 1490 us -> 1820 us (1.22)
  waiting for transfers between devices: 460 us -> 736 us
  other arithmetic: 410 us -> 467 us
    all_gather x0 -> x8, waiting for transfers between devices: none -> 735 us  [from_root(): return jnp.sum(lax.all_gather(kept, axis), axis=0)]
    psum x6 -> x0, waiting for transfers between devices: 460 us -> none  [from_root(): return lax.psum(kept, axis)]
    reduce_sum x0 -> x8, other arithmetic: none -> 59.4 us  [from_root(): return jnp.sum(lax.all_gather(kept, axis), axis=0)]
    unnamed x62 -> x54, local copies, waits for them, and re-layouts: 68.5 us -> 68.2 us
  transfers between devices with their start and end apart: 7 -> 9, of which waited for: 6 -> 8; matrix products, arithmetic and copies ran while one was open for 1% -> 2% of each run, Pallas kernels for 0% -> 0%
where the time goes in v1:
time: 1820 us; the launch traced here: 1810 us
  waiting for transfers between devices  736 us (40%)
  other arithmetic  467 us (26%)
  blocking collectives  264 us (15%)
  local copies, waits for them, and re-layouts  219 us (12%)
  matrix products  89.7 us (5%)
  between operations  22.9 us (1%)
    all_gather x8, waiting for transfers between devices, from_root(): return jnp.sum(lax.all_gather(kept, axis), axis=0)  735 us
    all_gather x1, blocking collectives, on_device(): everyone = lax.all_gather(child_tiles, ('row', 'col'), axis=0, tiled=True)  264 us
    another operation x30, other arithmetic, on_device(): corner = from_root(jnp.linalg.cholesky(candidate), 'row', owner_row)  159 us
    another operation x7, other arithmetic, right_solve(): jax.scipy.linalg.solve_triangular(factor, right_block.T, lower=True)  124 us
    another operation x14, other arithmetic, eliminate_child(): corner = jnp.linalg.cholesky(matrix[:CP, :CP])  80.8 us
    unnamed x54, local copies, waits for them, and re-layouts  68.2 us
    reduce_sum x8, other arithmetic, from_root(): return jnp.sum(lax.all_gather(kept, axis), axis=0)  59.4 us
    gather x2, local copies, waits for them, and re-layouts, on_device(): jnp.take(jnp.take(update, picked_rows, axis=0), picked_rows, axis=1)  38.8 us
  transfers between devices with their start and end apart: 9, of which 8 were waited for; matrix products, arithmetic and copies ran while one was open for 2% of the time, Pallas kernels for 0%

profile of v1, /device:TPU:0, one launch (start us, length us, event | category | flops | bytes accessed | tf_op | source)
XLA Modules:
  0.0 1810.0 jit_solution(5490657240634147864)
XLA Ops:
  7.2 17.6 copy.87
  35.0 11.7 cholesky.374
  60.8 11.7 cholesky.393
  85.8 11.7 cholesky.414
  110.9 11.8 cholesky.431
  142.0 40.1 %custom-call.27 = f32[4,128,128]{1,2,0:T(8,128)S(1)} custom-call(f32[4,128,128]{2,1,0:T(8,128)} %copy-done.17), custom_call_target="InvertDiagBlocksLowerTriangular" | custom-call | tf_op jit(solution)/shard_map/jit(_solve_triangular)/triangular_solve | solution.py:32
  193.1 19.6 %slice_subtract_fusion = f32[1536,1536]{0,1:T(8,128)} fusion(f32[2048,2048]{0,1:T(8,128)} %bitcast.243, f32[128,1536]{1,0:T(8,128)S(1)} %fusion.95, f32[128,1536]{1,0:T(8,128)S(1)} %fusion.96, f32[128,1536]{1,0:T(8,128)S(1)} %fusion.98, f32[128,1536]{1,0:T(8,128)S(1)} %fusion.37), kind=kOutput, calls=%fused_computation.10 | convolution fusion | flops 14500233216 | bytes 22020096 | tf_op jit(solution)/shard_map/dot_general | solution.py:22
  222.3 18.0 gather_fusion
  250.2 12.6 copy.97
  262.8 21.1 %gather_fusion.1 = f32[2048,2048]{1,0:T(8,128)} fusion(f32[2048,1536]{0,1:T(8,128)} %copy.97, s32[2048]{0:T(1024)S(1)} %broadcast_clamp_fusion), kind=kCustom, calls=%fused_computation.1 | custom fusion | bytes 33562624 | tf_op jit(solution)/shard_map/jit(_take)/gather | solution.py:74
  283.9 14.2 copy.151
  298.1 17.7 copy.98
  339.4 263.6 %all-gather.8 = s32[128,1,12]{2,1,0:T(1,128)S(1)} all-gather(s32[1,1,12]{2,1,0:T(1,128)S(1)} %bitcast.257), channel_id=1, replica_groups=mesh['row'=16,'col'=8] {'row','col'}, dimensions={0}, use_global_device_ids=true | all-gather | bytes 6192 | tf_op jit(solution)/shard_map/all_gather | solution.py:89
  606.7 18.4 %copy.156 = f32[32,8,128,128]{3,1,2,0:T(8,128)} copy(f32[32,8,128,128]{3,2,1,0:T(8,128)} %bitcast.90) | data formatting | bytes 33554432
  625.1 17.5 copy.99
  663.9 11.7 cholesky.446
  688.1 11.7 cholesky.465
  712.8 11.7 cholesky.486
  736.4 12.1 cholesky.503
  752.8 107.7 %all-gather.18.cloned.1.call-done = f32[8192,512]{1,0:T(8,128)} async-done(((f32[512,512]{1,0:T(8,128)}), f32[8192,512]{1,0:T(8,128)}) %all-gather.18.cloned.1.call-update) | async-done | bytes 16777232 | tf_op jit(solution)/shard_map/all_gather | solution.py:18
  880.8 39.9 %custom-call.41 = f32[4,128,128]{1,2,0:T(8,128)} custom-call(f32[4,128,128]{2,1,0:T(8,128)S(1)} %get-tuple-element.26), custom_call_target="InvertDiagBlocksLowerTriangular" | custom-call | tf_op jit(solution)/shard_map/jit(_solve_triangular)/triangular_solve | solution.py:32
  939.1 49.4 %all-gather.20.cloned.1.call-done = f32[4096,512]{1,0:T(8,128)} async-done(((f32[512,512]{1,0:T(8,128)}), f32[4096,512]{1,0:T(8,128)}) %all-gather.20.cloned.1.call-update) | async-done | bytes 8388624 | tf_op jit(solution)/shard_map/all_gather | solution.py:18
  997.0 109.4 %all-gather.22.cloned.1.call-done = f32[8192,512]{1,0:T(8,128)} async-done(((f32[512,512]{1,0:T(8,128)}), f32[8192,512]{1,0:T(8,128)}) %all-gather.22.cloned.1.call-update) | async-done | bytes 16777232 | tf_op jit(solution)/shard_map/all_gather | solution.py:18
  1115.3 104.8 %all-gather.24.cloned.1.call-done = f32[8192,512]{1,0:T(8,128)} async-done(((f32[512,512]{1,0:T(8,128)}), f32[8192,512]{1,0:T(8,128)}) %all-gather.24.cloned.1.call-update) | async-done | bytes 16777232 | tf_op jit(solution)/shard_map/all_gather | solution.py:18
  1237.7 11.9 cholesky.518
  1262.1 11.7 cholesky.537
  1286.6 12.1 cholesky.558
  1326.9 111.0 %all-gather.26.cloned.1.call-done = f32[8192,512]{1,0:T(8,128)} async-done(((f32[512,512]{1,0:T(8,128)}), f32[8192,512]{1,0:T(8,128)}) %all-gather.26.cloned.1.call-update) | async-done | bytes 16777232 | tf_op jit(solution)/shard_map/all_gather | solution.py:18
  1454.6 40.2 %custom-call.45 = f32[4,128,128]{1,2,0:T(8,128)S(1)} custom-call(f32[4,128,128]{2,1,0:T(8,128)} %copy-done.18), custom_call_target="InvertDiagBlocksLowerTriangular" | custom-call | tf_op jit(solution)/shard_map/jit(_solve_triangular)/triangular_solve | solution.py:32
  1503.3 49.4 %all-gather.28.cloned.1.call-done = f32[4096,512]{1,0:T(8,128)} async-done(((f32[512,512]{1,0:T(8,128)}), f32[4096,512]{1,0:T(8,128)}) %all-gather.28.cloned.1.call-update) | async-done | bytes 8388624 | tf_op jit(solution)/shard_map/all_gather | solution.py:18
  1573.0 97.6 %all-gather.30.cloned.1.call-done = f32[8192,512]{1,0:T(8,128)} async-done(((f32[512,512]{1,0:T(8,128)}), f32[8192,512]{1,0:T(8,128)}) %all-gather.30.cloned.1.call-update) | async-done | bytes 16777232 | tf_op jit(solution)/shard_map/all_gather | solution.py:18
  1678.6 105.3 %all-gather.32.cloned.1.call-done = f32[8192,512]{1,0:T(8,128)} async-done(((f32[512,512]{1,0:T(8,128)}), f32[8192,512]{1,0:T(8,128)}) %all-gather.32.cloned.1.call-update) | async-done | bytes 16777232 | tf_op jit(solution)/shard_map/all_gather | solution.py:18
  (289 shorter events, 412.3 us)
Async XLA Ops:
  27.1 2.1 copy-start.21
  34.0 1.0 copy-start.13
  141.3 0.7 copy-start.17
  142.0 45.6 %copy-start.19 = (s32[4,2]{0,1:T(2,128)}, s32[4,2]{0,1:T(2,128)S(1)}, u32[]{:S(2)}) copy-start(s32[4,2]{0,1:T(2,128)S(1)} %get-tuple-element.291) | copy-start | bytes 100
  183.0 9.1 copy-start
  185.6 6.5 copy-start.2
  188.5 3.6 copy-start.5
  192.1 0.9 copy-start.7
  327.6 277.2 %copy-start.15 = (f32[512,1024]{1,0:T(8,128)S(1)}, f32[512,1024]{1,0:T(8,128)}, u32[]{:S(2)}) copy-start(f32[512,1024]{1,0:T(8,128)} %param.8) | copy-start | bytes 6291460
  327.6 279.0 %all-to-all-start = ((f32[128,2,128,128]{3,2,1,0:T(8,128)}), f32[128,2,128,128]{3,2,1,0:T(8,128)}, u32[]{:S(2)}, u32[]{:S(2)}) async-start(f32[128,2,128,128]{3,2,1,0:T(8,128)} %bitcast.236), calls=%async_computation | async-start | bytes 33554432 | tf_op jit(solution)/shard_map/all_to_all | solution.py:81
  339.3 521.2 %all-gather.18.cloned.1.call-start = ((), (), s32[]{:S(2)}) async-start(), calls=%async_computation.1 | async-start | bytes 17825792 | tf_op jit(solution)/shard_map/all_gather | solution.py:18
  662.9 1.0 copy-start.11
  752.8 235.7 %all-gather.20.cloned.1.call-start = ((), (), s32[]{:S(2)}) async-start(), calls=%async_computation.2 | async-start | bytes 9437184 | tf_op jit(solution)/shard_map/all_gather | solution.py:18
  860.6 9.0 copy-start.20
  924.8 2.8 copy-start.8
  927.6 0.7 copy-start.14
  939.0 167.4 %all-gather.22.cloned.1.call-start = ((), (), s32[]{:S(2)}) async-start(), calls=%async_computation.3 | async-start | bytes 17825792 | tf_op jit(solution)/shard_map/all_gather | solution.py:18
  994.6 225.5 %all-gather.24.cloned.1.call-start = ((), (), s32[]{:S(2)}) async-start(), calls=%async_computation.4 | async-start | bytes 17825792 | tf_op jit(solution)/shard_map/all_gather | solution.py:18
  995.2 442.7 %all-gather.26.cloned.1.call-start = ((), (), s32[]{:S(2)}) async-start(), calls=%async_computation.5 | async-start | bytes 17825792 | tf_op jit(solution)/shard_map/all_gather | solution.py:18
  1234.5 1.3 copy-start.4
  1236.7 1.0 copy-start.12
  1326.7 226.0 %all-gather.28.cloned.1.call-start = ((), (), s32[]{:S(2)}) async-start(), calls=%async_computation.6 | async-start | bytes 9437184 | tf_op jit(solution)/shard_map/all_gather | solution.py:18
  1453.9 0.7 copy-start.18
  1454.6 40.2 %copy-start.10 = (f32[512,512]{1,0:T(8,128)}, f32[512,512]{1,0:T(8,128)S(1)}, u32[]{:S(2)}) copy-start(f32[512,512]{1,0:T(8,128)S(1)} %get-tuple-element.289) | copy-start | bytes 3145732
  1494.8 3.4 copy-start.16
  1503.2 167.4 %all-gather.30.cloned.1.call-start = ((), (), s32[]{:S(2)}) async-start(), calls=%async_computation.7 | async-start | bytes 17825792 | tf_op jit(solution)/shard_map/all_gather | solution.py:18
  1557.1 5.3 copy-start.1
  1557.2 5.3 copy-start.3
  1557.2 5.3 copy-start.6
  1558.8 225.0 %all-gather.32.cloned.1.call-start = ((), (), s32[]{:S(2)}) async-start(), calls=%async_computation.8 | async-start | bytes 17825792 | tf_op jit(solution)/shard_map/all_gather | solution.py:18
  1562.5 1.5 copy-start.9
Sparse Core Ops, SparseCore 0:
  752.9 107.6 all-gather.17
  939.1 49.2 all-gather.19
  994.7 111.6 all-gather.21
  1109.0 111.0 all-gather.23
  1326.8 111.0 all-gather.25
  1503.4 49.2 all-gather.27
  1559.0 111.6 all-gather.29
  1672.8 111.0 all-gather.31
